TPU v7x, 32 devices: a whole 2x2x4 slice. The times are simulated.
32 devices in a mesh: dp: 16 (over z, y, x), mp: 2 (over core).
Axes of the slice: x: 2, y: 2, z: 4, core: 2. Of those that a mesh axis runs over, the one named last changes fastest.
Arguments:
- hidden_in: bfloat16 [8192, 768], P(('dp', 'mp')), may hold values from -6 to 6
- memory: bfloat16 [8192, 768], P(('dp', 'mp')), may hold values from -6 to 6
- output_grad: bfloat16 [8192, 768], P(('dp', 'mp')), may hold values from -6 to 6
- segment_ids: int32 [16, 512], P('dp'), may hold values from 0 to 3, never falling along the last dimension, each value on 1 to 384 neighbouring positions
- route_counts: int32 [16, 16], replicated, may hold values from 0 to 32, as said below
- norm_gains: bfloat16 [3, 768], replicated, may hold values from 0.5 to 1.5
- self_qkv: bfloat16 [3, 768, 768], P(None, None, 'mp'), may hold values from -0.109375 to 0.109375
- self_out: bfloat16 [768, 768], P('mp'), may hold values from -1.75 to 1.75
- cross_qkv: bfloat16 [3, 768, 768], P(None, None, 'mp'), may hold values from -0.109375 to 0.109375
- cross_out: bfloat16 [768, 768], P('mp'), may hold values from -1.75 to 1.75
- ff_in: bfloat16 [768, 3072], P(None, 'mp'), may hold values from -0.21875 to 0.21875
- ff_out: bfloat16 [3072, 768], P('mp'), may hold values from -0.109375 to 0.109375
- rel_bias: bfloat16 [32, 12], P(None, 'mp'), may hold values from -4 to 4
Outputs:
- block_out: bfloat16 [8192, 768], P(('dp', 'mp'))
- input_grad: bfloat16 [8192, 768], P(('dp', 'mp'))
- memory_grad: bfloat16 [8192, 768], P(('dp', 'mp'))
- gains_grad: float32 [3, 768], replicated
- bias_grad: float32 [32, 12], replicated
- self_qkv_grad: float32 [3, 768, 768], P(None, 'dp', 'mp')
- self_out_grad: float32 [768, 768], P('mp', 'dp')
- cross_qkv_grad: float32 [3, 768, 768], P(None, 'dp', 'mp')
- cross_out_grad: float32 [768, 768], P('mp', 'dp')
- ff_in_grad: float32 [768, 3072], P('dp', 'mp')
- ff_out_grad: float32 [3072, 768], P('mp', 'dp')
Inputs may be any that keep to these rules, and one draw needn't show every extreme that they name: route_counts[s, o] is the number of rows that each core of dp index s sends to the same core of dp index o; every row and every column of the table sums to 256. `segment_ids`: each row holds the example ids of one dp index's rows in the owners' layout; they start at 0 and never fall, and each of the 4 examples has 1 to 384 rows.
All inputs are finite; a program needn't handle non-finite values.
Results may differ from a plain program's by a relative error of at most 0.04.
The roundings to bfloat16 on the way count: a program that leaves them out, or rounds other values in their place, can miss the bound.
Values may be sent and summed in bfloat16 or wider, within the bound.
No kernel may reach another device: no remote copies, remote signals or barrier semaphores. Data moves between devices by JAX's collectives and lax.ppermute only.
A program may use at most 128 MiB of HBM per device.

v0:
```python
from functools import partial
from functools import reduce

import jax
import jax.numpy as jnp
import numpy as np
from jax import lax
from jax.sharding import PartitionSpec as P

HEAD_DIM = 64
MAX_DIST = 128


epsilon = 1e-06
score_rows = 512
masked_score = -1e30


def for_sending(array):

    def short(part):
        return part.astype(jnp.bfloat16) if part.dtype == jnp.float32 else part

    return jax.tree.map(short, array)


def bucket_edges(buckets, distance):
    exact_span = buckets // 2
    edge_list = []
    for offset in range(1, 4 * distance):
        if offset < exact_span:
            bucket_now = offset
        else:
            log_ratio = np.log(offset / exact_span) / np.log(distance / exact_span)
            bucket_now = min(buckets - 1, exact_span + int(log_ratio * (buckets - exact_span)))
        while len(edge_list) < bucket_now:
            edge_list.append(offset)
    return np.array(edge_list, dtype=np.int32)


def rms_norm(values, gain_row):
    scale = lax.rsqrt(jnp.mean(values * values, axis=-1, keepdims=True) + epsilon)
    return values * scale * gain_row


def norm_back(values, gain_row, upstream):
    unused_value, pull = jax.vjp(rms_norm, values, gain_row)
    return pull(upstream)


def pack_rows(source_rows, counts, capacity):
    peer_count = counts.shape[0]
    starts = jnp.cumsum(counts) - counts
    within = jnp.arange(capacity, dtype=jnp.int32)
    active_position = within[None, :] < counts[:, None]
    row_index = jnp.where(active_position, starts[:, None] + within[None, :], 0).reshape(-1)
    picked = jnp.take(source_rows, row_index, axis=0).reshape(
        peer_count, capacity, source_rows.shape[1]
    )
    return jnp.where(active_position[:, :, None], picked, jnp.zeros_like(picked))


def unpack_rows(buckets, counts, row_total):
    peer_count, capacity, feature_width = buckets.shape
    end_rows = jnp.cumsum(counts)
    positions = jnp.arange(row_total, dtype=jnp.int32)
    source_of = jnp.sum((positions[:, None] >= end_rows[None, :]).astype(jnp.int32), axis=1)
    within = positions - jnp.take(end_rows - counts, source_of)
    flat_index = source_of * capacity + within
    return jnp.take(buckets.reshape(peer_count * capacity, feature_width), flat_index, axis=0)


def split_heads(tensor):
    return tensor.reshape(tensor.shape[0], -1, HEAD_DIM)


def merge_heads(tensor):
    return tensor.reshape(tensor.shape[0], -1)


def gather_rows(values):
    return jax.tree.map(
        lambda part, own: part.astype(own.dtype),
        lax.all_gather(for_sending(values), "mp", axis=0, tiled=True),
        values,
    )


def gather_grads(values):
    return lax.all_gather(values, "mp", axis=0, tiled=True)


def branch_sum(inputs, weight):
    return lax.psum_scatter(
        jnp.dot(inputs, weight, preferred_element_type=jnp.float32),
        "mp",
        scatter_dimension=0,
        tiled=True,
    )


def input_sum(grad_pairs):
    term_list = [
        jnp.einsum("re,de->rd", row_grads, weight, preferred_element_type=jnp.float32)
        for row_grads, weight in grad_pairs
    ]
    return lax.psum_scatter(reduce(jnp.add, term_list), "mp", scatter_dimension=0, tiled=True)


def block_scores(query_block, keys, query_ids, key_ids, edges, relative_bias_lookup):
    scores = jnp.einsum("qhd,khd->hqk", query_block, keys, preferred_element_type=jnp.float32)
    allowed = query_ids[:, None] == key_ids[None, :]
    indicator_matrix = None
    if edges is not None:
        query_pos = jnp.arange(query_block.shape[0], dtype=jnp.int32)
        key_pos = jnp.arange(keys.shape[0], dtype=jnp.int32)
        distance = query_pos[:, None] - key_pos[None, :]
        allowed = allowed & (distance >= 0)
        bucket = jnp.searchsorted(jnp.asarray(edges), distance, side="right")
        indicator_matrix = (
            bucket[None]
            == jnp.arange(relative_bias_lookup.shape[0], dtype=jnp.int32)[:, None, None]
        ).astype(jnp.bfloat16)
        scores = scores + jnp.einsum(
            "rig,rx->xig",
            indicator_matrix,
            relative_bias_lookup,
            preferred_element_type=jnp.float32,
        )
    scores = jnp.where(allowed[None], scores, masked_score)
    return (scores, allowed, indicator_matrix)


def block_plan(row_total):
    block_count = max(1, row_total // score_rows)
    return (block_count, row_total // block_count)


def attention_forward(queries, keys, values, example_ids, edges, relative_bias_lookup):
    scores, allowed, indicator_matrix = block_scores(
        queries, keys, example_ids, example_ids, edges, relative_bias_lookup
    )
    peak = jnp.max(scores, axis=-1, keepdims=True)
    weights = jnp.exp(scores - peak)
    totals = jnp.sum(weights, axis=-1, keepdims=True)
    probs = (weights / totals).astype(jnp.bfloat16)
    outputs = jnp.einsum("hqk,khd->qhd", probs, values, preferred_element_type=jnp.float32).astype(
        jnp.bfloat16
    )
    log_totals = (peak + jnp.log(totals))[..., 0]
    return (outputs, log_totals)


def attention_backward(
    queries, keys, values, out_grad, log_totals, example_ids, edges, relative_bias_lookup
):
    block_count, block_size = block_plan(queries.shape[0])
    bias_grad = None
    if edges is not None:
        bias_grad = jnp.zeros(relative_bias_lookup.shape, jnp.float32)
    scores, allowed, indicator_matrix = block_scores(
        queries, keys, example_ids, example_ids, edges, relative_bias_lookup
    )
    probs = jnp.where(allowed[None], jnp.exp(scores - log_totals[:, 0:block_size, None]), 0.0)
    prob_grad = jnp.einsum("qhd,khd->hqk", out_grad, values, preferred_element_type=jnp.float32)
    value_grad = jnp.einsum(
        "hqk,qhd->khd", probs.astype(jnp.bfloat16), out_grad, preferred_element_type=jnp.float32
    )
    score_gradient = (
        probs * (prob_grad - jnp.sum(probs * prob_grad, axis=-1, keepdims=True))
    ).astype(jnp.bfloat16)
    query_grads = jnp.einsum(
        "hqk,khd->qhd", score_gradient, keys, preferred_element_type=jnp.float32
    ).astype(jnp.bfloat16)
    key_grad = jnp.einsum(
        "hqk,qhd->khd", score_gradient, queries, preferred_element_type=jnp.float32
    )
    if edges is not None:
        bias_grad = jnp.einsum(
            "gji,vji->vg", score_gradient, indicator_matrix, preferred_element_type=jnp.float32
        )
    return (query_grads, key_grad.astype(jnp.bfloat16), value_grad.astype(jnp.bfloat16), bias_grad)


def local(
    hidden_in,
    memory,
    output_grad,
    segment_ids,
    route_counts,
    norm_gains,
    self_qkv,
    self_out,
    cross_qkv,
    cross_out,
    ff_in,
    ff_out,
    rel_bias,
):
    dp_count = lax.axis_size("dp")
    my_index = lax.axis_index("dp")
    half_rows = hidden_in.shape[0]
    capacity = 2 * (half_rows // dp_count)
    sent_counts = lax.dynamic_index_in_dim(route_counts, my_index, 0, keepdims=False)
    taken_counts = lax.dynamic_index_in_dim(route_counts, my_index, 1, keepdims=False)
    arrived = (
        lax.all_to_all(
            pack_rows(hidden_in, sent_counts, capacity),
            "dp",
            split_axis=0,
            concat_axis=0,
            tiled=True,
        ),
        lax.all_to_all(
            pack_rows(memory, sent_counts, capacity), "dp", split_axis=0, concat_axis=0, tiled=True
        ),
    )
    local_rows = unpack_rows(arrived[0], taken_counts, half_rows)
    local_memory = unpack_rows(arrived[1], taken_counts, half_rows)
    example_ids = segment_ids[0]
    edges = bucket_edges(rel_bias.shape[0], MAX_DIST)
    gains = norm_gains.astype(jnp.float32)
    inputs32 = local_rows.astype(jnp.float32)
    full_one = gather_rows(rms_norm(inputs32, gains[0]).astype(jnp.bfloat16))
    self_proj = jnp.einsum(
        "rd,sde->sre", full_one, self_qkv, preferred_element_type=jnp.float32
    ).astype(jnp.bfloat16)
    self_query = split_heads(self_proj[0])
    self_key = split_heads(self_proj[1])
    self_value = split_heads(self_proj[2])
    self_mix, self_lse = attention_forward(
        self_query, self_key, self_value, example_ids, edges, rel_bias
    )
    self_mix = merge_heads(self_mix)
    hidden_one = inputs32 + branch_sum(self_mix, self_out)
    full_two, full_memory = gather_rows(
        (rms_norm(hidden_one, gains[1]).astype(jnp.bfloat16), local_memory)
    )
    cross_query = split_heads(
        jnp.dot(full_two, cross_qkv[0], preferred_element_type=jnp.float32).astype(jnp.bfloat16)
    )
    cross_kv = jnp.einsum(
        "rd,sde->sre", full_memory, cross_qkv[1:], preferred_element_type=jnp.float32
    ).astype(jnp.bfloat16)
    cross_key = split_heads(cross_kv[0])
    cross_value = split_heads(cross_kv[1])
    cross_mix, cross_lse = attention_forward(
        cross_query, cross_key, cross_value, example_ids, None, None
    )
    cross_mix = merge_heads(cross_mix)
    hidden_two = hidden_one + branch_sum(cross_mix, cross_out)
    full_three = gather_rows(rms_norm(hidden_two, gains[2]).astype(jnp.bfloat16))
    pre_act = jnp.dot(full_three, ff_in, preferred_element_type=jnp.float32)
    activated = jax.nn.gelu(pre_act, approximate=True).astype(jnp.bfloat16)
    block_out = hidden_two + branch_sum(activated, ff_out)
    grad_three = output_grad.astype(jnp.float32)
    ff_grad_full = gather_grads(output_grad)
    act_grad = jnp.einsum("rd,fd->rf", ff_grad_full, ff_out, preferred_element_type=jnp.float32)
    ff_out_grad = jnp.einsum(
        "rf,rd->fd", activated, ff_grad_full, preferred_element_type=jnp.float32
    )
    discarded_activation, gelu_pull = jax.vjp(partial(jax.nn.gelu, approximate=True), pre_act)
    pre_grad = gelu_pull(act_grad)[0].astype(jnp.bfloat16)
    ff_in_grad = jnp.einsum("rd,rf->df", full_three, pre_grad, preferred_element_type=jnp.float32)
    back_three, gain_three = norm_back(hidden_two, gains[2], input_sum(((pre_grad, ff_in),)))
    grad_two = grad_three + back_three
    cross_grad_full = gather_grads(grad_two.astype(jnp.bfloat16))
    cross_out_grad = jnp.einsum(
        "re,rd->ed", cross_mix, cross_grad_full, preferred_element_type=jnp.float32
    )
    cross_mix_grad = split_heads(
        jnp.einsum(
            "rd,ed->re", cross_grad_full, cross_out, preferred_element_type=jnp.float32
        ).astype(jnp.bfloat16)
    )
    cq_grad, cross_key_gradient, cv_grad, unused_bias = attention_backward(
        cross_query, cross_key, cross_value, cross_mix_grad, cross_lse, example_ids, None, None
    )
    cq_grad = merge_heads(cq_grad)
    cross_key_gradient = merge_heads(cross_key_gradient)
    cv_grad = merge_heads(cv_grad)
    cross_query_grad = jnp.einsum(
        "rd,re->de", full_two, cq_grad, preferred_element_type=jnp.float32
    )
    cross_kv_grad = jnp.einsum(
        "rd,sre->sde",
        full_memory,
        jnp.stack([cross_key_gradient, cv_grad]),
        preferred_element_type=jnp.float32,
    )
    cross_qkv_grad = jnp.concatenate([cross_query_grad[None], cross_kv_grad], axis=0)
    memory_part = input_sum(((cross_key_gradient, cross_qkv[1]), (cv_grad, cross_qkv[2])))
    back_two, gain_two = norm_back(hidden_one, gains[1], input_sum(((cq_grad, cross_qkv[0]),)))
    grad_one = grad_two + back_two
    self_grad_full = gather_grads(grad_one.astype(jnp.bfloat16))
    self_out_grad = jnp.einsum(
        "re,rd->ed", self_mix, self_grad_full, preferred_element_type=jnp.float32
    )
    self_mix_grad = split_heads(
        jnp.einsum(
            "rd,ed->re", self_grad_full, self_out, preferred_element_type=jnp.float32
        ).astype(jnp.bfloat16)
    )
    sq_grad, sk_grad, sv_grad, bias_part = attention_backward(
        self_query, self_key, self_value, self_mix_grad, self_lse, example_ids, edges, rel_bias
    )
    self_grads = jnp.stack([merge_heads(sq_grad), merge_heads(sk_grad), merge_heads(sv_grad)])
    self_qkv_grad = jnp.einsum(
        "rd,sre->sde", full_one, self_grads, preferred_element_type=jnp.float32
    )
    normed_one_grad = input_sum(
        ((self_grads[0], self_qkv[0]), (self_grads[1], self_qkv[1]), (self_grads[2], self_qkv[2]))
    )
    back_one, gain_one = norm_back(inputs32, gains[0], normed_one_grad)
    input_part = grad_one + back_one
    returned = (
        lax.all_to_all(
            pack_rows(input_part.astype(jnp.bfloat16), taken_counts, capacity),
            "dp",
            split_axis=0,
            concat_axis=0,
            tiled=True,
        ),
        lax.all_to_all(
            pack_rows(memory_part.astype(jnp.bfloat16), taken_counts, capacity),
            "dp",
            split_axis=0,
            concat_axis=0,
            tiled=True,
        ),
    )
    input_grad = unpack_rows(returned[0], sent_counts, half_rows)
    memory_grad = unpack_rows(returned[1], sent_counts, half_rows)
    (
        self_qkv_total,
        self_out_total,
        cross_qkv_total,
        cross_output_accumulated,
        ff_in_total,
        ff_out_total,
    ) = (
        lax.psum_scatter(self_qkv_grad, "dp", scatter_dimension=1, tiled=True),
        lax.psum_scatter(self_out_grad, "dp", scatter_dimension=1, tiled=True),
        lax.psum_scatter(cross_qkv_grad, "dp", scatter_dimension=1, tiled=True),
        lax.psum_scatter(cross_out_grad, "dp", scatter_dimension=1, tiled=True),
        lax.psum_scatter(ff_in_grad, "dp", scatter_dimension=0, tiled=True),
        lax.psum_scatter(ff_out_grad, "dp", scatter_dimension=1, tiled=True),
    )
    local_heads = rel_bias.shape[1]
    bias_full = jnp.zeros((rel_bias.shape[0], local_heads * lax.axis_size("mp")), jnp.float32)
    bias_full = lax.dynamic_update_slice_in_dim(
        bias_full, bias_part, lax.axis_index("mp") * local_heads, 1
    )
    gain_grads = jnp.stack([gain_one, gain_two, gain_three])
    gains_total, bias_total = lax.psum((gain_grads, bias_full), ("dp", "mp"))
    return (
        block_out.astype(jnp.bfloat16),
        input_grad,
        memory_grad,
        gains_total,
        bias_total,
        self_qkv_total,
        self_out_total,
        cross_qkv_total,
        cross_output_accumulated,
        ff_in_total,
        ff_out_total,
    )


def solution(mesh):
    in_specs = (
        P(("dp", "mp"), None),
        P(("dp", "mp"), None),
        P(("dp", "mp"), None),
        P("dp", None),
        P(),
        P(),
        P(None, None, "mp"),
        P("mp", None),
        P(None, None, "mp"),
        P("mp", None),
        P(None, "mp"),
        P("mp", None),
        P(None, "mp"),
    )
    out_specs = (
        P(("dp", "mp"), None),
        P(("dp", "mp"), None),
        P(("dp", "mp"), None),
        P(),
        P(),
        P(None, "dp", "mp"),
        P("mp", "dp"),
        P(None, "dp", "mp"),
        P("mp", "dp"),
        P("dp", "mp"),
        P("mp", "dp"),
    )
    return jax.shard_map(local, mesh=mesh, in_specs=in_specs, out_specs=out_specs, check_vma=False)
```

profile of v0, /device:TPU:0, one launch (start us, length us, event | category | flops | bytes accessed | tf_op | source)
XLA Modules:
  0.0 1135.7 jit_solution(18325927747471088760)
XLA Ops:
  18.2 8.4 all-to-all-start
  26.8 20.4 %while.31 = (s32[]{:T(128)}, u32[512,512]{1,0:T(8,128)}, u32[512,512]{1,0:T(8,128)S(1)}, s32[]{:T(128)}, s32[]{:T(128)}) while((s32[]{:T(128)}, u32[512,512]{1,0:T(8,128)}, u32[512,512]{1,0:T(8,128)S(1)}, s32[]{:T(128)}, s32[]{:T(128)}) %tuple.107), condition=%wide.region_5.9_spmd.clone.clone, body=%wide.region_4.8_spmd.sunk.clone.clone.sunk | while | flops 18087940 | bytes 4194375 | solution.py:119
  30.1 4.3 fusion.174
  34.3 4.3 fusion.174
  38.6 4.3 fusion.174
  42.9 4.3 fusion.174
  52.3 10.2 compare_and_fusion.2
  63.6 7.9 fusion.5
  80.8 4.5 fusion.113
  91.9 28.5 %all_to_all.20 = bf16[16,32,768]{2,1,0:T(8,128)(2,1)S(1)} all-to-all(bf16[16,32,768]{2,1,0:T(8,128)(2,1)} %get-tuple-element.199), channel_id=1, replica_groups=mesh['dp'=16,'mp'=2] {'dp'}, dimensions={0} | all-to-all | bytes 1572864 | tf_op jit(solution)/shard_map/all_to_all | solution.py:214
  148.1 4.8 fusion.116
  157.8 4.3 fusion.22
  166.8 8.2 reduce-scatter.18.cloned.1.call-done
  183.1 7.6 multiply_reduce_fusion.1
  190.7 4.7 multiply_convert_fusion.1
  200.8 5.8 fusion.104
  211.1 4.4 fusion.33
  229.8 7.5 multiply_reduce_fusion
  237.3 4.7 multiply_convert_fusion
  255.6 6.5 copy.96
  265.1 6.2 copy.94
  276.3 5.6 fusion.103
  299.3 47.3 %all_to_all.21 = bf16[16,32,768]{2,1,0:T(8,128)(2,1)S(1)} all-to-all(bf16[16,32,768]{2,1,0:T(8,128)(2,1)S(1)} %get-tuple-element.195), channel_id=1, replica_groups=mesh['dp'=16,'mp'=2] {'dp'}, dimensions={0} | all-to-all | bytes 1572864 | tf_op jit(solution)/shard_map/all_to_all | solution.py:324
  346.6 6.1 all-to-all-start.2
  354.7 10.4 compare_and_fusion
  365.1 7.8 fusion.47
  373.0 42.0 %all-reduce.2 = (f32[3,768]{1,0:T(4,128)}, f32[32,12]{0,1:T(8,128)}) all-reduce(f32[3,768]{1,0:T(4,128)S(1)} %pad_maximum_fusion.1, f32[32,12]{0,1:T(8,128)S(1)} %dynamic_update_slice.3), channel_id=1, replica_groups=mesh['dp'=16,'mp'=2] {'dp','mp'}, use_global_device_ids=true, to_apply=%region_28.32 | all-reduce | flops 2688 | bytes 21504 | tf_op jit(solution)/shard_map/psum | solution.py:355
  420.2 167.5 %all-reduce.6.cloned.1.call-done = (f32[3,768,384]{2,0,1:T(4,128)}, f32[3,768,384]{2,0,1:T(4,128)}) async-done(((f32[3,768,384]{2,0,1:T(4,128)}, f32[3,768,384]{2,0,1:T(4,128)}), (f32[3,768,384]{2,0,1:T(4,128)}, f32[3,768,384]{2,0,1:T(4,128)})) %all-reduce.6.cloned.1.call-update) | async-done | bytes 7077904
  590.3 126.1 %reduce-scatter.28.cloned.1.call-done = f32[384,48]{0,1:T(8,128)} async-done(((f32[384,768]{0,1:T(8,128)}), f32[384,48]{0,1:T(8,128)}) %reduce-scatter.28.cloned.1.call-update) | async-done | bytes 73744 | tf_op jit(solution)/shard_map/reduce_scatter | solution.py:345
  716.4 128.5 %reduce-scatter.26.cloned.1.call-done = f32[384,48]{0,1:T(8,128)} async-done(((f32[384,768]{0,1:T(8,128)}), f32[384,48]{0,1:T(8,128)}) %reduce-scatter.26.cloned.1.call-update) | async-done | bytes 73744 | tf_op jit(solution)/shard_map/reduce_scatter | solution.py:343
  844.9 142.6 %reduce-scatter.32.cloned.1.call-done = f32[1536,48]{0,1:T(8,128)} async-done(((f32[1536,768]{0,1:T(8,128)}), f32[1536,48]{0,1:T(8,128)}) %reduce-scatter.32.cloned.1.call-update) | async-done | bytes 294928 | tf_op jit(solution)/shard_map/reduce_scatter | solution.py:347
  987.5 141.2 %reduce-scatter.30.cloned.1.call-done = f32[48,1536]{1,0:T(8,128)} async-done(((f32[768,1536]{1,0:T(8,128)}), f32[48,1536]{1,0:T(8,128)}) %reduce-scatter.30.cloned.1.call-update) | async-done | bytes 294928 | tf_op jit(solution)/shard_map/reduce_scatter | solution.py:346
  (366 shorter events, 152.9 us)
Async XLA Ops:
  7.2 150.6 %copy-start = (bf16[768,1536]{1,0:T(8,128)(2,1)S(1)}, bf16[768,1536]{1,0:T(8,128)(2,1)}, u32[]{:S(2)}) copy-start(bf16[768,1536]{1,0:T(8,128)(2,1)} %param.32) | copy-start | bytes 7077892
  16.8 9.9 copy-start.92
  18.2 53.3 %all-to-all-start = ((bf16[16,32,768]{2,1,0:T(8,128)(2,1)}), bf16[16,32,768]{2,1,0:T(8,128)(2,1)}, u32[]{:S(2)}, u32[]{:S(2)}) async-start(bf16[16,32,768]{2,1,0:T(8,128)(2,1)} %get-tuple-element.200), calls=%async_computation | async-start | bytes 1572864 | tf_op jit(solution)/shard_map/all_to_all | solution.py:207
  26.6 103.2 %reduce-scatter.12.cloned.1.call-start = ((), (), s32[]{:S(2)}) async-start(), calls=%async_computation.15 | async-start | bytes 2359296 | tf_op jit(solution)/shard_map/reduce_scatter | solution.py:94
  47.1 15.5 %copy-start.90 = (s32[1,512]{1,0:T(1,128)S(1)}, s32[1,512]{1,0:T(1,128)}, u32[]{:S(2)}) copy-start(s32[1,512]{1,0:T(1,128)} %param.25) | copy-start | bytes 6148
  47.1 16.5 %copy-start.99 = (bf16[32,6]{0,1:T(8,128)(2,1)S(1)}, bf16[32,6]{0,1:T(8,128)(2,1)}, u32[]{:S(2)}) copy-start(bf16[32,6]{0,1:T(8,128)(2,1)} %param.34) | copy-start | bytes 1156
  51.5 20.0 %copy-start.93 = (s32[16]{0:T(128)}, s32[16]{0:T(128)S(1)}, u32[]{:S(2)}) copy-start(s32[16]{0:T(128)S(1)} %get-tuple-element.163) | copy-start | bytes 196
  62.5 12.0 %copy-start.75 = (pred[256]{0:T(512)(128)(4,1)}, pred[256]{0:T(512)(128)(4,1)S(1)}, u32[]{:S(2)}) copy-start(pred[256]{0:T(512)(128)(4,1)S(1)} %get-tuple-element.183) | copy-start | bytes 772
  63.6 17.1 %copy-start.10 = (pred[512,512]{0,1:T(8,128)(4,1)}, pred[512,512]{0,1:T(8,128)(4,1)S(1)}, u32[]{:S(2)}) copy-start(pred[512,512]{0,1:T(8,128)(4,1)S(1)} %get-tuple-element.198) | copy-start | bytes 786436
  91.8 61.1 %reduce-scatter.14.cloned.1.call-start = ((), (), s32[]{:S(2)}) async-start(), calls=%async_computation.16 | async-start | bytes 2359296 | tf_op jit(solution)/shard_map/reduce_scatter | solution.py:94
  144.6 30.4 %reduce-scatter.18.cloned.1.call-start = ((), (), s32[]{:S(2)}) async-start(), calls=%async_computation.18 | async-start | bytes 2359296 | tf_op jit(solution)/shard_map/reduce_scatter | solution.py:107
  165.8 11.3 copy-start.88
  165.8 11.4 copy-start.9
  165.8 11.4 %copy-start.22 = (bf16[256,768]{1,0:T(8,128)(2,1)S(1)}, bf16[256,768]{1,0:T(8,128)(2,1)}, u32[]{:S(2)}) copy-start(bf16[256,768]{1,0:T(8,128)(2,1)} %param.24) | copy-start | bytes 1179652
  165.9 11.4 %copy-start.74 = (f32[256]{0:T(256)S(1)}, f32[256]{0:T(256)}, u32[]{:S(2)}) copy-start(f32[256]{0:T(256)} %copy-done.73) | copy-start | bytes 3076
  165.9 52.3 %reduce-scatter.20.cloned.1.call-start = ((), (), s32[]{:S(2)}) async-start(), calls=%async_computation.19 | async-start | bytes 2359296 | tf_op jit(solution)/shard_map/reduce_scatter | solution.py:107
  166.8 16.3 %copy-start.15 = (pred[512,512]{0,1:T(8,128)(4,1)S(1)}, pred[512,512]{0,1:T(8,128)(4,1)}, u32[]{:S(2)}) copy-start(pred[512,512]{0,1:T(8,128)(4,1)} %get-tuple-element.197) | copy-start | bytes 786436
  200.7 22.8 %reduce-scatter.16.cloned.1.call-start = ((), (), s32[]{:S(2)}) async-start(), calls=%async_computation.17 | async-start | bytes 2359296 | tf_op jit(solution)/shard_map/reduce_scatter | solution.py:94
  206.6 82.5 %reduce-scatter.24.cloned.1.call-start = ((), (), s32[]{:S(2)}) async-start(), calls=%async_computation.21 | async-start | bytes 2359296 | tf_op jit(solution)/shard_map/reduce_scatter | solution.py:107
  218.1 74.4 %reduce-scatter.22.cloned.1.call-start = ((), (), s32[]{:S(2)}) async-start(), calls=%async_computation.20 | async-start | bytes 2359296 | tf_op jit(solution)/shard_map/reduce_scatter | solution.py:107
  250.5 337.2 %all-reduce.6.cloned.1.call-start = ((), (), s32[]{:S(2)}) async-start(), calls=%async_computation.26 | async-start | bytes 18874368
  271.4 445.0 %reduce-scatter.28.cloned.1.call-start = ((), (), s32[]{:S(2)}) async-start(), calls=%async_computation.23 | async-start | bytes 1253376 | tf_op jit(solution)/shard_map/reduce_scatter | solution.py:345
  274.3 570.7 %reduce-scatter.26.cloned.1.call-start = ((), (), s32[]{:S(2)}) async-start(), calls=%async_computation.22 | async-start | bytes 1253376 | tf_op jit(solution)/shard_map/reduce_scatter | solution.py:343
  276.1 711.4 %reduce-scatter.32.cloned.1.call-start = ((), (), s32[]{:S(2)}) async-start(), calls=%async_computation.25 | async-start | bytes 5013504 | tf_op jit(solution)/shard_map/reduce_scatter | solution.py:347
  281.9 846.7 %reduce-scatter.30.cloned.1.call-start = ((), (), s32[]{:S(2)}) async-start(), calls=%async_computation.24 | async-start | bytes 5013504 | tf_op jit(solution)/shard_map/reduce_scatter | solution.py:346
  298.1 54.5 %copy-start.100 = (u32[32]{0:T(128)S(1)}, u32[32]{0:T(128)}, u32[]{:S(2)}) copy-start(u32[32]{0:T(128)} %constant.354) | copy-start | bytes 388
  298.1 56.5 %copy-start.96 = (s32[16]{0:T(128)S(1)}, s32[16]{0:T(128)}, u32[]{:S(2)}) copy-start(s32[16]{0:T(128)} %copy-done.95) | copy-start | bytes 196
  298.1 66.9 %copy-start.77 = (f32[768]{0:T(1024)S(1)}, f32[768]{0:T(1024)}, u32[]{:S(2)}) copy-start(f32[768]{0:T(1024)} %get-tuple-element.155) | copy-start | bytes 9220
  298.1 66.9 %copy-start.78 = (f32[768]{0:T(1024)S(1)}, f32[768]{0:T(1024)}, u32[]{:S(2)}) copy-start(f32[768]{0:T(1024)} %get-tuple-element.153) | copy-start | bytes 9220
  298.2 67.0 %copy-start.12 = (s32[512,512]{0,1:T(8,128)S(1)}, s32[512,512]{0,1:T(8,128)}, u32[]{:S(2)}) copy-start(s32[512,512]{0,1:T(8,128)} %copy.82) | copy-start | bytes 3145732
  346.6 69.7 %all-to-all-start.2 = ((bf16[16,32,768]{2,1,0:T(8,128)(2,1)}), bf16[16,32,768]{2,1,0:T(8,128)(2,1)S(1)}, u32[]{:S(2)}, u32[]{:S(2)}) async-start(bf16[16,32,768]{2,1,0:T(8,128)(2,1)} %get-tuple-element.196), calls=%async_computation.8 | async-start | bytes 1572864 | tf_op jit(solution)/shard_map/all_to_all | solution.py:317
  416.3 712.4 %copy-start.1 = (bf16[768,1536]{1,0:T(8,128)(2,1)S(1)}, bf16[768,1536]{1,0:T(8,128)(2,1)}, u32[]{:S(2)}) copy-start(bf16[768,1536]{1,0:T(8,128)(2,1)} %param.32) | copy-start | bytes 7077892
  (88 other events, 340.9 us)
Sparse Core Ops, SparseCore 0:
  91.9 10.2 reduce-scatter.11
  144.7 6.8 reduce-scatter.13
  166.0 8.9 reduce-scatter.17
  200.9 10.2 reduce-scatter.19
  213.2 10.2 reduce-scatter.15
  225.7 10.2 reduce-scatter.23
  250.7 10.2 reduce-scatter.21
  271.5 316.1 all-reduce.5
  593.8 122.5 reduce-scatter.27
  722.3 122.5 reduce-scatter.25
  851.5 135.9 reduce-scatter.31
  993.1 135.5 reduce-scatter.29
where the time goes:
time: 1140 us
  waiting for transfers between devices  718 us (63%)
  blocking collectives  136 us (12%)
  matrix products  108 us (9%)
  other arithmetic  83.9 us (7%)
  local copies, waits for them, and re-layouts  58.7 us (5%)
  between operations  16.5 us (1%)
  starting transfers between devices  15.1 us (1%)
    unnamed x13, waiting for transfers between devices  168 us
    reduce_scatter x1, waiting for transfers between devices, local(): lax.psum_scatter(ff_out_grad, 'dp', scatter_dimension=1, tiled=True)  143 us
    reduce_scatter x1, waiting for transfers between devices, local(): lax.psum_scatter(ff_in_grad, 'dp', scatter_dimension=0, tiled=True)  141 us
    reduce_scatter x1, waiting for transfers between devices, local(): lax.psum_scatter(self_out_grad, 'dp', scatter_dimension=1, tiled=True)  129 us
    reduce_scatter x1, waiting for transfers between devices, local(): lax.psum_scatter(cross_out_grad, 'dp', scatter_dimension=1, tiled=True)  126 us
    all_to_all x1, blocking collectives, local(): lax.all_to_all(pack_rows(memory_part.astype(jnp.bfloat16), taken_counts,...  47.3 us
    psum x1, blocking collectives, local(): gains_total, bias_total = lax.psum((gain_grads, bias_full), ('dp', 'mp'))  42 us
    all_to_all x1, blocking collectives, local(): lax.all_to_all(pack_rows(memory, sent_counts, capacity), 'dp', split_axis...  28.5 us
  transfers between devices with their start and end apart: 14, of which 7 were waited for; matrix products, arithmetic and copies ran while one was open for 15% of the time, Pallas kernels for 0%

commit v1 on v0

v1 whole, which is shorter than its diff:
```python
from functools import partial

import jax
import jax.numpy as jnp
import numpy as np
from jax import lax
from jax.sharding import PartitionSpec as P

HEAD_DIM = 64
MAX_DIST = 128
EPS = 1e-06
MASKED = -1e30
F32 = jnp.float32
BF16 = jnp.bfloat16


def bucket_edges(buckets, distance):
    exact_span = buckets // 2
    edge_list = []
    for offset in range(1, 4 * distance):
        if offset < exact_span:
            bucket_now = offset
        else:
            log_ratio = np.log(offset / exact_span) / np.log(distance / exact_span)
            bucket_now = min(buckets - 1, exact_span + int(log_ratio * (buckets - exact_span)))
        while len(edge_list) < bucket_now:
            edge_list.append(offset)
    return np.array(edge_list, dtype=np.int32)


def dot(a, b):
    return jnp.dot(a, b, preferred_element_type=F32)


def dot_nt(a, b):
    return lax.dot_general(a, b, (((1,), (1,)), ((), ())), preferred_element_type=F32)


def dot_tn(a, b):
    return lax.dot_general(a, b, (((0,), (0,)), ((), ())), preferred_element_type=F32)


def rms_norm(values, gain_row):
    scale = lax.rsqrt(jnp.mean(values * values, axis=-1, keepdims=True) + EPS)
    return values * scale * gain_row


def norm_back(values, gain_row, upstream):
    scale = lax.rsqrt(jnp.mean(values * values, axis=-1, keepdims=True) + EPS)
    scaled = gain_row * upstream
    back = scale * scaled - values * (
        scale * scale * scale * jnp.mean(scaled * values, axis=-1, keepdims=True)
    )
    return back, upstream * values * scale


def slot_matrix(counts, capacity, row_total):
    peers = counts.shape[0]
    order = jnp.arange(peers, dtype=jnp.int32)
    starts = jnp.sum(jnp.where(order[None, :] < order[:, None], counts[None, :], 0), axis=1)
    within = jnp.arange(capacity, dtype=jnp.int32)
    rows = jnp.where(within[None, :] < counts[:, None], starts[:, None] + within[None, :], -1)
    return (
        rows.reshape(-1)[:, None] == jnp.arange(row_total, dtype=jnp.int32)[None, :]
    ).astype(BF16)


def exchange_rows(packed, peers):
    shape = packed.shape
    blocks = packed.reshape(peers, shape[0] // peers, shape[1])
    return lax.all_to_all(blocks, "dp", split_axis=0, concat_axis=0, tiled=True).reshape(shape)


def swap(values):
    return lax.ppermute(values, "mp", [(0, 1), (1, 0)])


def neighbour(values, bit, peers):
    return lax.ppermute(values, "dp", [(i, i ^ (1 << bit)) for i in range(peers)])


def order_matrix(order, peers, me, width):
    size = width // peers
    row = lax.broadcasted_iota(jnp.int32, (width, width), 0)
    column = lax.broadcasted_iota(jnp.int32, (width, width), 1)
    block, within = row // size, row % size
    relative = jnp.zeros_like(block)
    steps = len(order)
    for position, bit in enumerate(order):
        relative = relative + (((block >> (steps - 1 - position)) & 1) << bit)
    return (column == (relative ^ me) * size + within).astype(BF16)


def halve(grads, order, peers):
    for bit in order:
        half = grads.shape[0] // 2
        arrived = neighbour(grads[half:], bit, peers)
        grads = (grads[:half].astype(F32) + arrived.astype(F32)).astype(BF16)
    return grads


def local(
    hidden_in,
    memory,
    output_grad,
    segment_ids,
    route_counts,
    norm_gains,
    self_qkv,
    self_out,
    cross_qkv,
    cross_out,
    ff_in,
    ff_out,
    rel_bias,
):
    peers = lax.axis_size("dp")
    me = lax.axis_index("dp")
    core = lax.axis_index("mp")
    half_rows, width = hidden_in.shape
    rows = 2 * half_rows
    capacity = 2 * (half_rows // peers)
    heads = rel_bias.shape[1]
    bits = peers.bit_length() - 1
    order_a = tuple(range(bits))
    order_b = (1, 0) + tuple(range(2, bits))

    def own(values):
        return lax.dynamic_slice_in_dim(values, core * half_rows, half_rows, 0)

    def both(values):
        return lax.all_gather(values, "mp", axis=0, tiled=True)

    sent = lax.dynamic_index_in_dim(route_counts, me, 0, keepdims=False)
    taken = lax.dynamic_index_in_dim(route_counts, me, 1, keepdims=False)
    send_slots = slot_matrix(sent, capacity, half_rows)
    take_slots = slot_matrix(taken, capacity, half_rows)

    def there(values):
        arrived = exchange_rows(dot(send_slots, values).astype(BF16), peers)
        return dot_tn(take_slots, arrived).astype(BF16)

    def back(values):
        arrived = exchange_rows(dot(take_slots, values).astype(BF16), peers)
        return dot_tn(send_slots, arrived).astype(BF16)

    x_full = both(there(hidden_in))
    mem_full = both(there(memory))
    og_full = both(output_grad)

    perm_a = order_matrix(order_a, peers, me, width)
    perm_b = order_matrix(order_b, peers, me, width)

    def left_a(values):
        return dot_nt(perm_a, values).astype(BF16)

    def left_b(values):
        return dot_nt(perm_b, values).astype(BF16)

    gains = norm_gains.astype(F32)
    ids = segment_ids[0]
    position = jnp.arange(rows, dtype=jnp.int32)
    distance = position[:, None] - position[None, :]
    same = ids[:, None] == ids[None, :]
    causal = same & (distance >= 0)
    edges = bucket_edges(rel_bias.shape[0], MAX_DIST)
    bucket = jnp.zeros_like(distance)
    for edge in edges.tolist():
        bucket = bucket + (distance >= edge).astype(jnp.int32)
    indicator = (
        bucket[None] == jnp.arange(rel_bias.shape[0], dtype=jnp.int32)[:, None, None]
    ).astype(BF16)
    bias_grid = jnp.einsum("bij,bh->hij", indicator, rel_bias, preferred_element_type=F32)

    def split(values):
        return values.reshape(rows, -1, HEAD_DIM)

    def merge(values):
        return values.reshape(rows, -1)

    def attend(q, k, v, allowed, bias):
        scores = jnp.einsum("qhd,khd->hqk", split(q), split(k), preferred_element_type=F32)
        if bias is not None:
            scores = scores + bias
        scores = jnp.where(allowed[None], scores, MASKED)
        peak = jnp.max(scores, axis=-1, keepdims=True)
        weights = jnp.exp(scores - peak)
        probs = weights / jnp.sum(weights, axis=-1, keepdims=True)
        mix = jnp.einsum("hqk,khd->qhd", probs.astype(BF16), split(v), preferred_element_type=F32)
        return merge(mix).astype(BF16), probs

    def attend_back(q, k, v, probs, d_mix):
        d_mix = split(d_mix)
        d_probs = jnp.einsum("qhd,khd->hqk", d_mix, split(v), preferred_element_type=F32)
        dv = jnp.einsum("hqk,qhd->khd", probs.astype(BF16), d_mix, preferred_element_type=F32)
        d_scores = (
            probs * (d_probs - jnp.sum(probs * d_probs, axis=-1, keepdims=True))
        ).astype(BF16)
        dq = jnp.einsum("hqk,khd->qhd", d_scores, split(k), preferred_element_type=F32)
        dk = jnp.einsum("hqk,qhd->khd", d_scores, split(q), preferred_element_type=F32)
        return (
            merge(dq).astype(BF16),
            merge(dk).astype(BF16),
            merge(dv).astype(BF16),
            d_scores,
        )

    def branch(partial_sum):
        kept = partial_sum.astype(BF16)
        return kept.astype(F32) + swap(kept).astype(F32)

    x = x_full.astype(F32)
    n1 = rms_norm(x, gains[0]).astype(BF16)
    sq, sk, sv = (dot(n1, self_qkv[i]).astype(BF16) for i in range(3))
    self_mix, self_probs = attend(sq, sk, sv, causal, bias_grid)
    h1 = x + branch(dot(self_mix, self_out))
    n2 = rms_norm(h1, gains[1]).astype(BF16)
    cq = dot(n2, cross_qkv[0]).astype(BF16)
    ck, cv = (dot(mem_full, cross_qkv[i]).astype(BF16) for i in (1, 2))
    cross_mix, cross_probs = attend(cq, ck, cv, same, None)
    h2 = h1 + branch(dot(cross_mix, cross_out))
    n3 = rms_norm(h2, gains[2]).astype(BF16)
    pre = dot(n3, ff_in)
    d_act = dot_nt(og_full, ff_out)
    act, gelu_pull = jax.vjp(partial(jax.nn.gelu, approximate=True), pre)
    act = act.astype(BF16)
    d_pre = gelu_pull(d_act)[0].astype(BF16)
    block_out = own(h2) + branch_own(dot(act, ff_out), core, half_rows)

    middle = act.shape[1] // 2
    ff_out_a = halve(dot(left_a(og_full), act[:, :middle]).astype(BF16), order_a, peers)
    ff_out_b = halve(dot(left_b(og_full), act[:, middle:]).astype(BF16), order_b, peers)
    ff_in_a = halve(dot(left_a(n3), d_pre[:, :middle]).astype(BF16), order_a, peers)
    ff_in_b = halve(dot(left_b(n3), d_pre[:, middle:]).astype(BF16), order_b, peers)

    dn3 = branch(dot_nt(d_pre, ff_in))
    dv3, gain3 = norm_back(h2, gains[2], dn3)
    g2 = og_full.astype(F32) + dv3
    g2s = g2.astype(BF16)
    d_cmix = dot_nt(g2s, cross_out).astype(BF16)
    dcq, dck, dcv, unused = attend_back(cq, ck, cv, cross_probs, d_cmix)
    dcols = dcq.shape[1]
    cross_a = halve(
        jnp.concatenate([dot(left_a(g2s), cross_mix), dot(left_a(n2), dcq)], axis=1).astype(BF16),
        order_a,
        peers,
    )
    cross_b = halve(
        dot(left_b(mem_full), jnp.concatenate([dck, dcv], axis=1)).astype(BF16), order_b, peers
    )
    d_mem = branch_own(dot_nt(dck, cross_qkv[1]) + dot_nt(dcv, cross_qkv[2]), core, half_rows)
    memory_grad = back(d_mem.astype(BF16))
    dn2 = branch(dot_nt(dcq, cross_qkv[0]))
    dv2, gain2 = norm_back(h1, gains[1], dn2)
    g1 = g2 + dv2
    g1s = g1.astype(BF16)
    d_smix = dot_nt(g1s, self_out).astype(BF16)
    dsq, dsk, dsv, d_scores = attend_back(sq, sk, sv, self_probs, d_smix)
    self_a = halve(
        jnp.concatenate([dot(left_a(g1s), self_mix), dot(left_a(n1), dsq)], axis=1).astype(BF16),
        order_a,
        peers,
    )
    self_b = halve(
        dot(left_b(n1), jnp.concatenate([dsk, dsv], axis=1)).astype(BF16), order_b, peers
    )
    bias_part = jnp.einsum("hij,bij->bh", d_scores, indicator, preferred_element_type=F32)
    dn1 = branch_own(
        dot_nt(dsq, self_qkv[0]) + dot_nt(dsk, self_qkv[1]) + dot_nt(dsv, self_qkv[2]),
        core,
        half_rows,
    )
    dv1, gain1 = norm_back(own(x), gains[0], dn1)
    input_grad = back((own(g1) + dv1).astype(BF16))

    small = jnp.zeros((rel_bias.shape[0], heads * 2), F32)
    small = lax.dynamic_update_slice_in_dim(small, bias_part, core * heads, 1)
    gain_rows = jnp.stack(
        [jnp.sum(gain1, axis=0), jnp.sum(own(gain2), axis=0), jnp.sum(own(gain3), axis=0)]
    )
    small = jnp.concatenate([gain_rows.reshape(-1), small.reshape(-1)])
    small = small + swap(small)
    for bit in order_a:
        small = small + neighbour(small, bit, peers)
    gains_total = small[: 3 * width].reshape(3, width)
    bias_total = small[3 * width :].reshape(rel_bias.shape[0], heads * 2)

    ff_out_total = jnp.concatenate([ff_out_a, ff_out_b], axis=1).astype(F32).T
    ff_in_total = jnp.concatenate([ff_in_a, ff_in_b], axis=1).astype(F32)
    cross_out_total = cross_a[:, :dcols].astype(F32).T
    cross_qkv_total = jnp.stack([cross_a[:, dcols:], cross_b[:, :dcols], cross_b[:, dcols:]])
    self_out_total = self_a[:, :dcols].astype(F32).T
    self_qkv_total = jnp.stack([self_a[:, dcols:], self_b[:, :dcols], self_b[:, dcols:]])
    return (
        block_out.astype(BF16),
        input_grad,
        memory_grad,
        gains_total,
        bias_total,
        self_qkv_total.astype(F32),
        self_out_total,
        cross_qkv_total.astype(F32),
        cross_out_total,
        ff_in_total,
        ff_out_total,
    )


def branch_own(partial_sum, core, half_rows):
    kept = lax.dynamic_slice_in_dim(partial_sum, core * half_rows, half_rows, 0)
    sent = lax.dynamic_slice_in_dim(partial_sum, (1 - core) * half_rows, half_rows, 0)
    return kept + swap(sent.astype(BF16)).astype(F32)


def solution(mesh):
    both = ("dp", "mp")
    in_specs = (
        P(both, None),
        P(both, None),
        P(both, None),
        P("dp", None),
        P(),
        P(),
        P(None, None, "mp"),
        P("mp", None),
        P(None, None, "mp"),
        P("mp", None),
        P(None, "mp"),
        P("mp", None),
        P(None, "mp"),
    )
    out_specs = (
        P(both, None),
        P(both, None),
        P(both, None),
        P(),
        P(),
        P(None, "dp", "mp"),
        P("mp", "dp"),
        P(None, "dp", "mp"),
        P("mp", "dp"),
        P("dp", "mp"),
        P("mp", "dp"),
    )
    return jax.shard_map(local, mesh=mesh, in_specs=in_specs, out_specs=out_specs, check_vma=False)
```

time: 1140 us -> 427 us (0.37)
  waiting for transfers between devices: 718 us -> 81.3 us
  blocking collectives: 136 us -> 7.52 us
  starting transfers between devices: 15.1 us -> 78.3 us
  matrix products: 108 us -> 145 us
  other arithmetic: 83.9 us -> 52.1 us
  between operations: 16.5 us -> 2.6 us
    reduce_scatter x11 -> x0, waiting for transfers between devices: 550 us -> none  [the longest x1 143 us: local(): lax.psum_scatter(ff_out_grad, 'dp', scatter_dimension=1, tiled=True)]
    unnamed x13 -> x0, waiting for transfers between devices: 168 us -> none
    ppermute x0 -> x44, waiting for transfers between devices: none -> 81.3 us  [the longest x36 79.9 us: neighbour(): return lax.ppermute(values, 'dp', [(i, i ^ 1 << bit) for i in range(peers)])]
    all_to_all x2 -> x0, blocking collectives: 75.7 us -> none  [the longest x1 47.3 us: local(): lax.all_to_all(pack_rows(memory_part.astype(jnp.bfloat16), taken_counts,...]
    ppermute x0 -> x44, starting transfers between devices: none -> 50.2 us  [the longest x36 48.7 us: neighbour(): return lax.ppermute(values, 'dp', [(i, i ^ 1 << bit) for i in range(peers)])]
    psum x1 -> x0, blocking collectives: 42 us -> none  [local(): gains_total, bias_total = lax.psum((gain_grads, bias_full), ('dp', 'mp'))]
    dot_general x38 -> x51, matrix products: 108 us -> 138 us  [the longest x24 63.2 us: dot(): return jnp.dot(a, b, preferred_element_type=F32)]
    select_n x15 -> x2, other arithmetic: 27.6 us -> 0.15 us  [slot_matrix(): jnp.where(within[None, :] < counts[:, None], starts[:, None] + within[Non...]
  transfers between devices with their start and end apart: 14 -> 48, of which waited for: 7 -> 22; matrix products, arithmetic and copies ran while one was open for 15% -> 47% of each run, Pallas kernels for 0% -> 0%
where the time goes in v1:
time: 427 us; the launch traced here: 420 us
  matrix products  145 us (34%)
  waiting for transfers between devices  81.3 us (19%)
  starting transfers between devices  78.3 us (18%)
  local copies, waits for them, and re-layouts  53.3 us (12%)
  other arithmetic  52.1 us (12%)
  blocking collectives  7.52 us (2%)
    ppermute x36, waiting for transfers between devices, neighbour(): return lax.ppermute(values, 'dp', [(i, i ^ 1 << bit) for i in range(peers)])  79.9 us
    dot_general x24, matrix products, dot(): return jnp.dot(a, b, preferred_element_type=F32)  63.2 us
    ppermute x36, starting transfers between devices, neighbour(): return lax.ppermute(values, 'dp', [(i, i ^ 1 << bit) for i in range(peers)])  48.7 us
    all_to_all x4, starting transfers between devices, exchange_rows(): lax.all_to_all(blocks, 'dp', split_axis=0, concat_axis=0, tiled=True)  28.2 us
    dot_general x10, matrix products, dot_nt(): lax.dot_general(a, b, (((1,), (1,)), ((), ())), preferred_element_type=F32)  21.7 us
    convert_element_type x32, other arithmetic, halve(): grads = (grads[:half].astype(F32) + arrived.astype(F32)).astype(BF16)  17.8 us
    slice x30, local copies, waits for them, and re-layouts, halve(): arrived = neighbour(grads[half:], bit, peers)  12.9 us
    dot_general x2, matrix products, attend_back(): jnp.einsum('hqk,qhd->khd', probs.astype(BF16), d_mix, preferred_element_t...  12.1 us
  transfers between devices with their start and end apart: 48, of which 22 were waited for; matrix products, arithmetic and copies ran while one was open for 47% of the time, Pallas kernels for 0%

profile of v1, /device:TPU:0, one launch (start us, length us, event | category | flops | bytes accessed | tf_op | source)
XLA Modules:
  0.0 419.7 jit_solution(6178170671948252139)
XLA Ops:
  4.1 8.5 %all-to-all-start = ((bf16[16,32,768]{2,1,0:T(8,128)(2,1)}), bf16[16,32,768]{2,1,0:T(8,128)(2,1)}, u32[]{:S(2)}, u32[]{:S(2)}) async-start(bf16[16,32,768]{2,1,0:T(8,128)(2,1)} %bitcast.1), calls=%async_computation | async-start | bytes 1572864 | tf_op jit(solution)/shard_map/all_to_all | solution.py:71
  16.5 7.2 %fusion.3 = f32[512,512,6]{1,2,0:T(8,128)} fusion(s32[512,512]{1,0:T(8,128)S(1)} %copy.77, bf16[32,6]{0,1:T(8,128)(2,1)S(1)} %copy-done.103), kind=kOutput, calls=%fused_computation.4 | convolution fusion | flops 109051904 | bytes 7340416 | tf_op jit(solution)/shard_map/bij,bh->hij/dot_general | solution.py:173
  23.6 9.1 %copy.78 = f32[512,512,6]{0,1,2:T(8,128)} copy(f32[512,512,6]{1,2,0:T(8,128)} %fusion.3) | data formatting | bytes 12582912 | tf_op jit(solution)/shard_map/bij,bh->hij/dot_general | solution.py:173
  37.9 6.9 %all-to-all-start.1 = ((bf16[16,32,768]{2,1,0:T(8,128)(2,1)}), bf16[16,32,768]{2,1,0:T(8,128)(2,1)}, u32[]{:S(2)}, u32[]{:S(2)}) async-start(bf16[16,32,768]{2,1,0:T(8,128)(2,1)} %bitcast.14), calls=%async_computation.1 | async-start | bytes 1572864 | tf_op jit(solution)/shard_map/all_to_all | solution.py:71
  53.9 4.5 %fusion.193 = (f32[6,512]{1,0:T(8,128)}, f32[6,512,512]{1,2,0:T(8,128)}) fusion(f32[6,512,512]{1,2,0:T(8,128)S(1)} %fusion.6), kind=kOutput, calls=%fused_computation.333 | output fusion | flops 3146239 | bytes 12595200 | tf_op jit(solution)/shard_map/sub | solution.py:187
  58.5 6.5 %fusion.49 = bf16[6,64,512]{2,1,0:T(8,128)(2,1)S(1)} fusion(bf16[512,6,64]{0,2,1:T(8,128)(2,1)} %bitcast.200, f32[6,512]{1,0:T(8,128)} %get-tuple-element.82, f32[6,512,512]{1,2,0:T(8,128)} %copy-done.10), kind=kOutput, calls=%fused_computation.111 | convolution fusion | flops 206245376 | bytes 7090176 | tf_op jit(solution)/shard_map/hqk,khd->qhd/dot_general | solution.py:189
  78.1 6.7 %fusion.194 = (f32[6,512]{1,0:T(8,128)}, f32[6,512,512]{1,2,0:T(8,128)}) fusion(pred[512,512]{0,1:T(8,128)(4,1)} %get-tuple-element.80, bf16[512,6,64]{0,2,1:T(8,128)(2,1)S(1)} %bitcast.178, bf16[512,6,64]{0,2,1:T(8,128)(2,1)} %bitcast.194), kind=kOutput, calls=%fused_computation.334 | convolution fusion | flops 206045696 | bytes 7352320 | tf_op jit(solution)/shard_map/sub | solution.py:187
  97.2 4.9 %fusion.16 = (bf16[512,1536]{1,0:T(8,128)(2,1)}, bf16[512,1536]{1,0:T(8,128)(2,1)}) fusion(f32[512,1536]{1,0:T(8,128)S(1)} %fusion.196, bf16[512,768]{1,0:T(8,128)(2,1)S(1)} %multiply_convert_fusion.3, bf16[768,1536]{1,0:T(8,128)(2,1)S(1)} %copy-done), kind=kOutput, calls=%fused_computation.31 | convolution fusion | flops 1225261056 | bytes 9437184 | tf_op jit(solution)/shard_map/dot_general | solution.py:32
  102.1 4.4 %convolution_convert_fusion.2 = bf16[768,768]{1,0:T(8,128)(2,1)} fusion(bf16[512,768]{1,0:T(8,128)(2,1)} %copy-done.65, bf16[512,1536]{1,0:T(8,128)(2,1)} %get-tuple-element.64, s32[768]{0:T(1024)} %get-tuple-element.93, s32[768]{0:T(1024)} %get-tuple-element.94, s32[]{:T(128)S(6)} %axis_index.23, s32[768]{0:T(1024)} %get-tuple-element.92, ...), kind=kOutput, calls=%fused_computation.84 | convolution fusion | flops 1221328896 | bytes 2770948 | tf_op jit(solution)/shard_map/dot_general | solution.py:32
  106.5 4.4 %convolution_convert_fusion.3 = bf16[768,768]{1,0:T(8,128)(2,1)} fusion(bf16[512,768]{1,0:T(8,128)(2,1)} %copy-done.65, bf16[512,1536]{1,0:T(8,128)(2,1)} %get-tuple-element.64, s32[768]{0:T(1024)} %get-tuple-element.93, s32[768]{0:T(1024)} %get-tuple-element.94, s32[]{:T(128)S(6)} %axis_index.23, s32[768]{0:T(1024)} %get-tuple-element.92, ...), kind=kOutput, calls=%fused_computation.85 | convolution fusion | flops 1221328896 | bytes 2770948 | tf_op jit(solution)/shard_map/dot_general | solution.py:32
  110.9 4.4 %convolution_convert_fusion = bf16[768,768]{1,0:T(8,128)(2,1)} fusion(bf16[512,768]{1,0:T(8,128)(2,1)} %copy-done.27, bf16[512,1536]{1,0:T(8,128)(2,1)} %get-tuple-element.65, s32[768]{0:T(1024)} %get-tuple-element.93, s32[768]{0:T(1024)} %get-tuple-element.94, s32[]{:T(128)S(6)} %axis_index.23, s32[768]{0:T(1024)} %get-tuple-element.92, ...), kind=kOutput, calls=%fused_computation.82 | convolution fusion | flops 1221328896 | bytes 2770948 | tf_op jit(solution)/shard_map/dot_general | solution.py:32
  115.3 4.4 %convolution_convert_fusion.1 = bf16[768,768]{1,0:T(8,128)(2,1)} fusion(bf16[512,768]{1,0:T(8,128)(2,1)} %copy-done.27, bf16[512,1536]{1,0:T(8,128)(2,1)} %get-tuple-element.65, s32[768]{0:T(1024)} %get-tuple-element.93, s32[768]{0:T(1024)} %get-tuple-element.94, s32[]{:T(128)S(6)} %axis_index.23, s32[768]{0:T(1024)} %get-tuple-element.92, ...), kind=kOutput, calls=%fused_computation.83 | convolution fusion | flops 1221328896 | bytes 2770948 | tf_op jit(solution)/shard_map/dot_general | solution.py:32
  131.4 5.7 %collective-permute-done.32 = bf16[384,768]{1,0:T(8,128)(2,1)S(1)} collective-permute-done((bf16[384,768]{1,0:T(8,128)(2,1)S(1)}, bf16[384,768]{1,0:T(8,128)(2,1)S(1)}, u32[]{:S(2)}, u32[]{:S(2)}) %collective-permute-start.32) | collective-permute-done | bytes 589856 | tf_op jit(solution)/shard_map/ppermute | solution.py:79
  145.1 4.2 %collective-permute-done.40 = bf16[384,768]{1,0:T(8,128)(2,1)S(1)} collective-permute-done((bf16[384,768]{1,0:T(8,128)(2,1)S(1)}, bf16[384,768]{1,0:T(8,128)(2,1)S(1)}, u32[]{:S(2)}, u32[]{:S(2)}) %collective-permute-start.40) | collective-permute-done | bytes 589856 | tf_op jit(solution)/shard_map/ppermute | solution.py:79
  160.8 4.3 %convolution_convert_fusion.25 = bf16[768,384]{0,1:T(8,128)(2,1)} fusion(bf16[512,384]{0,1:T(8,128)(2,1)} %bitcast.187, f32[512,768]{1,0:T(8,128)} %get-tuple-element.71, s32[768]{0:T(1024)} %get-tuple-element.93, s32[768]{0:T(1024)} %get-tuple-element.94, s32[]{:T(128)S(6)} %axis_index.23, s32[768]{0:T(1024)} %get-tuple-element.92, ...), kind=kOutput, calls=%fused_computation.108 | convolution fusion | flops 919437312 | bytes 2569732 | tf_op jit(solution)/shard_map/dot_general | solution.py:32
  165.6 4.9 %fusion.58 = bf16[6,64,512]{2,1,0:T(8,128)(2,1)} fusion(bf16[512,6,64]{0,2,1:T(8,128)(2,1)S(1)} %bitcast.192, f32[6,512,512]{1,2,0:T(8,128)} %get-tuple-element.85, f32[6,512]{1,0:T(8,128)S(1)} %copy-done.86), kind=kOutput, calls=%fused_computation.114 | convolution fusion | flops 204668928 | bytes 7090176 | tf_op jit(solution)/shard_map/hqk,qhd->khd/dot_general | solution.py:195
  178.1 4.3 %convolution_convert_fusion.4 = bf16[768,768]{1,0:T(8,128)(2,1)} fusion(bf16[512,768]{1,0:T(8,128)(2,1)} %copy-done.64, bf16[512,384]{0,1:T(8,128)(2,1)S(1)} %bitcast.196, bf16[512,384]{0,1:T(8,128)(2,1)S(1)} %bitcast.175, s32[768]{0:T(1024)} %get-tuple-element.93, s32[768]{0:T(1024)} %get-tuple-element.94, s32[]{:T(128)S(6)} %axis_index.23, ...), kind=kOutput, calls=%fused_computation.86 | convolution fusion | flops 1222901760 | bytes 2766340 | tf_op jit(solution)/shard_map/dot_general | solution.py:32
  218.5 4.5 %collective-permute-done.38 = bf16[96,768]{1,0:T(8,128)(2,1)S(1)} collective-permute-done((bf16[96,768]{1,0:T(8,128)(2,1)S(1)}, bf16[96,768]{1,0:T(8,128)(2,1)S(1)}, u32[]{:S(2)}, u32[]{:S(2)}) %collective-permute-start.38) | collective-permute-done | bytes 147488 | tf_op jit(solution)/shard_map/ppermute | solution.py:79
  225.4 4.4 %collective-permute-done.35 = bf16[48,768]{1,0:T(8,128)(2,1)S(1)} collective-permute-done((bf16[48,768]{1,0:T(8,128)(2,1)S(1)}, bf16[48,768]{1,0:T(8,128)(2,1)S(1)}, u32[]{:S(2)}, u32[]{:S(2)}) %collective-permute-start.35) | collective-permute-done | bytes 73760 | tf_op jit(solution)/shard_map/ppermute | solution.py:79
  230.6 6.2 %collective-permute-done.31 = bf16[48,768]{1,0:T(8,128)(2,1)S(1)} collective-permute-done((bf16[48,768]{1,0:T(8,128)(2,1)S(1)}, bf16[48,768]{1,0:T(8,128)(2,1)S(1)}, u32[]{:S(2)}, u32[]{:S(2)}) %collective-permute-start.31) | collective-permute-done | bytes 73760 | tf_op jit(solution)/shard_map/ppermute | solution.py:79
  237.6 4.6 %collective-permute-done.43 = bf16[48,768]{1,0:T(8,128)(2,1)S(1)} collective-permute-done((bf16[48,768]{1,0:T(8,128)(2,1)S(1)}, bf16[48,768]{1,0:T(8,128)(2,1)S(1)}, u32[]{:S(2)}, u32[]{:S(2)}) %collective-permute-start.43) | collective-permute-done | bytes 73760 | tf_op jit(solution)/shard_map/ppermute | solution.py:79
  242.3 5.2 %collective-permute-done.39 = bf16[48,768]{1,0:T(8,128)(2,1)S(1)} collective-permute-done((bf16[48,768]{1,0:T(8,128)(2,1)S(1)}, bf16[48,768]{1,0:T(8,128)(2,1)S(1)}, u32[]{:S(2)}, u32[]{:S(2)}) %collective-permute-start.39) | collective-permute-done | bytes 73760 | tf_op jit(solution)/shard_map/ppermute | solution.py:79
  249.6 5.0 %all-to-all-start.3 = ((bf16[16,32,768]{2,1,0:T(8,128)(2,1)}), bf16[16,32,768]{2,1,0:T(8,128)(2,1)}, u32[]{:S(2)}, u32[]{:S(2)}) async-start(bf16[16,32,768]{2,1,0:T(8,128)(2,1)} %bitcast.168), calls=%async_computation.3 | async-start | bytes 1572864 | tf_op jit(solution)/shard_map/all_to_all | solution.py:71
  274.1 7.2 %fusion.52 = bf16[6,64,512]{2,1,0:T(8,128)(2,1)} fusion(bf16[512,6,64]{0,2,1:T(8,128)(2,1)S(1)} %bitcast.190, f32[6,512]{1,0:T(8,128)S(1)} %copy-done.74, f32[6,512,512]{1,2,0:T(8,128)} %copy-done.10), kind=kOutput, calls=%fused_computation.112 | convolution fusion | flops 206245376 | bytes 7090176 | tf_op jit(solution)/shard_map/hqk,qhd->khd/dot_general | solution.py:195
  290.1 8.2 %copy.87 = bf16[6,512,512]{2,0,1:T(8,128)(2,1)} copy(bf16[6,512,512]{1,2,0:T(8,128)(2,1)} %copy-done.2) | data formatting | bytes 6291456 | tf_op jit(solution)/shard_map/convert_element_type | solution.py:198
  306.6 4.1 convolution_convert_fusion.5
  315.4 6.9 %fusion.61 = f32[32,6]{1,0:T(8,128)S(1)} fusion(bf16[6,512,512]{2,0,1:T(8,128)(2,1)} %copy.87, s32[512,512]{1,0:T(8,128)S(1)} %copy-done.20), kind=kOutput, calls=%fused_computation.143 | convolution fusion | flops 109051904 | bytes 4195072 | tf_op jit(solution)/shard_map/hij,bij->bh/dot_general | solution.py:267
  333.4 4.4 %collective-permute-done.22 = bf16[96,768]{0,1:T(8,128)(2,1)S(1)} collective-permute-done((bf16[96,768]{0,1:T(8,128)(2,1)S(1)}, bf16[96,768]{0,1:T(8,128)(2,1)S(1)}, u32[]{:S(2)}, u32[]{:S(2)}) %collective-permute-start.22) | collective-permute-done | bytes 147488 | tf_op jit(solution)/shard_map/ppermute | solution.py:79
  343.8 8.0 %collective-permute-done.23 = bf16[48,768]{0,1:T(8,128)(2,1)S(1)} collective-permute-done((bf16[48,768]{0,1:T(8,128)(2,1)S(1)}, bf16[48,768]{0,1:T(8,128)(2,1)S(1)}, u32[]{:S(2)}, u32[]{:S(2)}) %collective-permute-start.23) | collective-permute-done | bytes 73760 | tf_op jit(solution)/shard_map/ppermute | solution.py:79
  388.9 7.8 %all-to-all-start.2 = ((bf16[16,32,768]{2,1,0:T(8,128)(2,1)}), bf16[16,32,768]{2,1,0:T(8,128)(2,1)S(1)}, u32[]{:S(2)}, u32[]{:S(2)}) async-start(bf16[16,32,768]{2,1,0:T(8,128)(2,1)} %bitcast.34), calls=%async_computation.2 | async-start | bytes 1572864 | tf_op jit(solution)/shard_map/all_to_all | solution.py:71
  403.8 5.2 %collective-permute-done.15 = bf16[48,768]{0,1:T(8,128)(2,1)} collective-permute-done((bf16[48,768]{0,1:T(8,128)(2,1)}, bf16[48,768]{0,1:T(8,128)(2,1)}, u32[]{:S(2)}, u32[]{:S(2)}) %collective-permute-start.15) | collective-permute-done | bytes 73760 | tf_op jit(solution)/shard_map/ppermute | solution.py:79
  412.3 4.4 %collective-permute-done.19 = bf16[48,768]{1,0:T(8,128)(2,1)} collective-permute-done((bf16[48,768]{1,0:T(8,128)(2,1)}, bf16[48,768]{1,0:T(8,128)(2,1)}, u32[]{:S(2)}, u32[]{:S(2)}) %collective-permute-start.19) | collective-permute-done | bytes 73760 | tf_op jit(solution)/shard_map/ppermute | solution.py:79
  (493 shorter events, 235.8 us)
Async XLA Ops:
  4.1 33.8 %all-to-all-start = ((bf16[16,32,768]{2,1,0:T(8,128)(2,1)}), bf16[16,32,768]{2,1,0:T(8,128)(2,1)}, u32[]{:S(2)}, u32[]{:S(2)}) async-start(bf16[16,32,768]{2,1,0:T(8,128)(2,1)} %bitcast.1), calls=%async_computation | async-start | bytes 1572864 | tf_op jit(solution)/shard_map/all_to_all | solution.py:71
  37.9 29.9 %all-to-all-start.1 = ((bf16[16,32,768]{2,1,0:T(8,128)(2,1)}), bf16[16,32,768]{2,1,0:T(8,128)(2,1)}, u32[]{:S(2)}, u32[]{:S(2)}) async-start(bf16[16,32,768]{2,1,0:T(8,128)(2,1)} %bitcast.14), calls=%async_computation.1 | async-start | bytes 1572864 | tf_op jit(solution)/shard_map/all_to_all | solution.py:71
  120.9 16.2 %collective-permute-start.32 = (bf16[384,768]{1,0:T(8,128)(2,1)S(1)}, bf16[384,768]{1,0:T(8,128)(2,1)S(1)}, u32[]{:S(2)}, u32[]{:S(2)}) collective-permute-start(bf16[384,768]{1,0:T(8,128)(2,1)S(1)} %slice.424), channel_id=1, source_target_pairs={{0,4},{2,6},{4,0},{6,2},{8,12},{10,14},{12,8},{14,10},{16,20},{18,... | collective-permute-start | bytes 1769480 | tf_op jit(solution)/shard_map/ppermute | solution.py:79
  125.7 16.2 %collective-permute-start.28 = (bf16[384,768]{1,0:T(8,128)(2,1)S(1)}, bf16[384,768]{1,0:T(8,128)(2,1)S(1)}, u32[]{:S(2)}, u32[]{:S(2)}) collective-permute-start(bf16[384,768]{1,0:T(8,128)(2,1)S(1)} %slice.415), channel_id=1, source_target_pairs={{0,2},{2,0},{4,6},{6,4},{8,10},{10,8},{12,14},{14,12},{16,18},{18,... | collective-permute-start | bytes 1769480 | tf_op jit(solution)/shard_map/ppermute | solution.py:79
  129.3 27.6 %collective-permute-start.3 = (bf16[512,768]{1,0:T(8,128)(2,1)S(1)}, bf16[512,768]{1,0:T(8,128)(2,1)S(1)}, u32[]{:S(2)}, u32[]{:S(2)}) collective-permute-start(bf16[512,768]{1,0:T(8,128)(2,1)S(1)} %convolution_convert_fusion.18), channel_id=1, source_target_pairs={{0,1},{1,0},{2,3},{3,2},{4,5},{5,4},{6,7},{7,6},{8,9},{9,8},{10,11... | collective-permute-start | bytes 2359304 | tf_op jit(solution)/shard_map/ppermute | solution.py:75
  129.4 19.8 %collective-permute-start.40 = (bf16[384,768]{1,0:T(8,128)(2,1)S(1)}, bf16[384,768]{1,0:T(8,128)(2,1)S(1)}, u32[]{:S(2)}, u32[]{:S(2)}) collective-permute-start(bf16[384,768]{1,0:T(8,128)(2,1)S(1)} %slice.442), channel_id=1, source_target_pairs={{0,4},{2,6},{4,0},{6,2},{8,12},{10,14},{12,8},{14,10},{16,20},{18,... | collective-permute-start | bytes 1769480 | tf_op jit(solution)/shard_map/ppermute | solution.py:79
  131.1 60.2 %collective-permute-start.2 = (bf16[256,768]{1,0:T(8,128)(2,1)}, bf16[256,768]{1,0:T(8,128)(2,1)}, u32[]{:S(2)}, u32[]{:S(2)}) collective-permute-start(bf16[256,768]{1,0:T(8,128)(2,1)} %dynamic-slice_convert_fusion.2), channel_id=1, source_target_pairs={{0,1},{1,0},{2,3},{3,2},{4,5},{5,4},{6,7},{7,6},{8,9},{9,8},{10,11... | collective-permute-start | bytes 1179656 | tf_op jit(solution)/shard_map/ppermute | solution.py:75
  137.1 17.5 %collective-permute-start.36 = (bf16[384,768]{1,0:T(8,128)(2,1)S(1)}, bf16[384,768]{1,0:T(8,128)(2,1)S(1)}, u32[]{:S(2)}, u32[]{:S(2)}) collective-permute-start(bf16[384,768]{1,0:T(8,128)(2,1)S(1)} %slice.433), channel_id=1, source_target_pairs={{0,2},{2,0},{4,6},{6,4},{8,10},{10,8},{12,14},{14,12},{16,18},{18,... | collective-permute-start | bytes 1769480 | tf_op jit(solution)/shard_map/ppermute | solution.py:79
  142.0 54.1 %collective-permute-start.33 = (bf16[192,768]{1,0:T(8,128)(2,1)}, bf16[192,768]{1,0:T(8,128)(2,1)}, u32[]{:S(2)}, u32[]{:S(2)}) collective-permute-start(bf16[192,768]{1,0:T(8,128)(2,1)} %slice.426), channel_id=1, source_target_pairs={{0,2},{2,0},{4,6},{6,4},{8,10},{10,8},{12,14},{14,12},{16,18},{18,... | collective-permute-start | bytes 884744 | tf_op jit(solution)/shard_map/ppermute | solution.py:79
  149.3 48.4 %collective-permute-start.29 = (bf16[192,768]{1,0:T(8,128)(2,1)}, bf16[192,768]{1,0:T(8,128)(2,1)}, u32[]{:S(2)}, u32[]{:S(2)}) collective-permute-start(bf16[192,768]{1,0:T(8,128)(2,1)} %slice.417), channel_id=1, source_target_pairs={{0,4},{2,6},{4,0},{6,2},{8,12},{10,14},{12,8},{14,10},{16,20},{18,... | collective-permute-start | bytes 884744 | tf_op jit(solution)/shard_map/ppermute | solution.py:79
  154.6 44.3 %collective-permute-start.41 = (bf16[192,768]{1,0:T(8,128)(2,1)}, bf16[192,768]{1,0:T(8,128)(2,1)}, u32[]{:S(2)}, u32[]{:S(2)}) collective-permute-start(bf16[192,768]{1,0:T(8,128)(2,1)} %slice.444), channel_id=1, source_target_pairs={{0,2},{2,0},{4,6},{6,4},{8,10},{10,8},{12,14},{14,12},{16,18},{18,... | collective-permute-start | bytes 884744 | tf_op jit(solution)/shard_map/ppermute | solution.py:79
  157.1 43.6 %collective-permute-start.37 = (bf16[192,768]{1,0:T(8,128)(2,1)}, bf16[192,768]{1,0:T(8,128)(2,1)}, u32[]{:S(2)}, u32[]{:S(2)}) collective-permute-start(bf16[192,768]{1,0:T(8,128)(2,1)} %slice.435), channel_id=1, source_target_pairs={{0,4},{2,6},{4,0},{6,2},{8,12},{10,14},{12,8},{14,10},{16,20},{18,... | collective-permute-start | bytes 884744 | tf_op jit(solution)/shard_map/ppermute | solution.py:79
  191.4 63.2 %collective-permute-start.24 = (bf16[384,768]{1,0:T(8,128)(2,1)}, bf16[384,768]{1,0:T(8,128)(2,1)}, u32[]{:S(2)}, u32[]{:S(2)}) collective-permute-start(bf16[384,768]{1,0:T(8,128)(2,1)} %slice.403), channel_id=1, source_target_pairs={{0,4},{2,6},{4,0},{6,2},{8,12},{10,14},{12,8},{14,10},{16,20},{18,... | collective-permute-start | bytes 1769480 | tf_op jit(solution)/shard_map/ppermute | solution.py:79
  196.1 62.7 %collective-permute-start.20 = (bf16[384,768]{0,1:T(8,128)(2,1)}, bf16[384,768]{0,1:T(8,128)(2,1)}, u32[]{:S(2)}, u32[]{:S(2)}) collective-permute-start(bf16[384,768]{0,1:T(8,128)(2,1)} %pad_maximum_fusion), channel_id=1, source_target_pairs={{0,2},{2,0},{4,6},{6,4},{8,10},{10,8},{12,14},{14,12},{16,18},{18,... | collective-permute-start | bytes 1769480 | tf_op jit(solution)/shard_map/ppermute | solution.py:79
  197.7 65.6 %collective-permute-start.4 = (bf16[512,768]{1,0:T(8,128)(2,1)S(1)}, bf16[512,768]{1,0:T(8,128)(2,1)}, u32[]{:S(2)}, u32[]{:S(2)}) collective-permute-start(bf16[512,768]{1,0:T(8,128)(2,1)S(1)} %convolution_convert_fusion.21), channel_id=1, source_target_pairs={{0,1},{1,0},{2,3},{3,2},{4,5},{5,4},{6,7},{7,6},{8,9},{9,8},{10,11... | collective-permute-start | bytes 2359304 | tf_op jit(solution)/shard_map/ppermute | solution.py:75
  198.9 49.4 %collective-permute-start.6 = (bf16[256,768]{1,0:T(8,128)(2,1)S(1)}, bf16[256,768]{1,0:T(8,128)(2,1)S(1)}, u32[]{:S(2)}, u32[]{:S(2)}) collective-permute-start(bf16[256,768]{1,0:T(8,128)(2,1)S(1)} %dynamic-slice_convert_fusion), channel_id=1, source_target_pairs={{0,1},{1,0},{2,3},{3,2},{4,5},{5,4},{6,7},{7,6},{8,9},{9,8},{10,11... | collective-permute-start | bytes 1179656 | tf_op jit(solution)/shard_map/ppermute | solution.py:75
  249.6 139.3 %all-to-all-start.3 = ((bf16[16,32,768]{2,1,0:T(8,128)(2,1)}), bf16[16,32,768]{2,1,0:T(8,128)(2,1)}, u32[]{:S(2)}, u32[]{:S(2)}) async-start(bf16[16,32,768]{2,1,0:T(8,128)(2,1)} %bitcast.168), calls=%async_computation.3 | async-start | bytes 1572864 | tf_op jit(solution)/shard_map/all_to_all | solution.py:71
  256.9 75.0 %collective-permute-start.25 = (bf16[192,768]{1,0:T(8,128)(2,1)}, bf16[192,768]{1,0:T(8,128)(2,1)}, u32[]{:S(2)}, u32[]{:S(2)}) collective-permute-start(bf16[192,768]{1,0:T(8,128)(2,1)} %slice.405), channel_id=1, source_target_pairs={{0,2},{2,0},{4,6},{6,4},{8,10},{10,8},{12,14},{14,12},{16,18},{18,... | collective-permute-start | bytes 884744 | tf_op jit(solution)/shard_map/ppermute | solution.py:79
  261.8 66.9 %collective-permute-start.21 = (bf16[192,768]{0,1:T(8,128)(2,1)}, bf16[192,768]{0,1:T(8,128)(2,1)}, u32[]{:S(2)}, u32[]{:S(2)}) collective-permute-start(bf16[192,768]{0,1:T(8,128)(2,1)} %slice.396), channel_id=1, source_target_pairs={{0,4},{2,6},{4,0},{6,2},{8,12},{10,14},{12,8},{14,10},{16,20},{18,... | collective-permute-start | bytes 884744 | tf_op jit(solution)/shard_map/ppermute | solution.py:79
  314.7 55.4 %collective-permute-start.12 = (bf16[384,768]{0,1:T(8,128)(2,1)}, bf16[384,768]{0,1:T(8,128)(2,1)}, u32[]{:S(2)}, u32[]{:S(2)}) collective-permute-start(bf16[384,768]{0,1:T(8,128)(2,1)} %pad_maximum_fusion.1), channel_id=1, source_target_pairs={{0,2},{2,0},{4,6},{6,4},{8,10},{10,8},{12,14},{14,12},{16,18},{18,... | collective-permute-start | bytes 1769480 | tf_op jit(solution)/shard_map/ppermute | solution.py:79
  315.2 57.7 %collective-permute-start.16 = (bf16[384,768]{1,0:T(8,128)(2,1)}, bf16[384,768]{1,0:T(8,128)(2,1)}, u32[]{:S(2)}, u32[]{:S(2)}) collective-permute-start(bf16[384,768]{1,0:T(8,128)(2,1)} %slice.383), channel_id=1, source_target_pairs={{0,4},{2,6},{4,0},{6,2},{8,12},{10,14},{12,8},{14,10},{16,20},{18,... | collective-permute-start | bytes 1769480 | tf_op jit(solution)/shard_map/ppermute | solution.py:79
  328.7 23.2 %collective-permute-start.5 = (bf16[256,768]{1,0:T(8,128)(2,1)}, bf16[256,768]{1,0:T(8,128)(2,1)S(1)}, u32[]{:S(2)}, u32[]{:S(2)}) collective-permute-start(bf16[256,768]{1,0:T(8,128)(2,1)} %dynamic-slice_convert_fusion.1), channel_id=1, source_target_pairs={{0,1},{1,0},{2,3},{3,2},{4,5},{5,4},{6,7},{7,6},{8,9},{9,8},{10,11... | collective-permute-start | bytes 1179656 | tf_op jit(solution)/shard_map/ppermute | solution.py:75
  329.9 7.8 %collective-permute-start.22 = (bf16[96,768]{0,1:T(8,128)(2,1)S(1)}, bf16[96,768]{0,1:T(8,128)(2,1)S(1)}, u32[]{:S(2)}, u32[]{:S(2)}) collective-permute-start(bf16[96,768]{0,1:T(8,128)(2,1)S(1)} %slice.398), channel_id=1, source_target_pairs={{0,8},{2,10},{4,12},{6,14},{8,0},{10,2},{12,4},{14,6},{16,24},{18,... | collective-permute-start | bytes 442376 | tf_op jit(solution)/shard_map/ppermute | solution.py:79
  338.0 13.8 %collective-permute-start.23 = (bf16[48,768]{0,1:T(8,128)(2,1)S(1)}, bf16[48,768]{0,1:T(8,128)(2,1)S(1)}, u32[]{:S(2)}, u32[]{:S(2)}) collective-permute-start(bf16[48,768]{0,1:T(8,128)(2,1)S(1)} %slice.400), channel_id=1, source_target_pairs={{0,16},{2,18},{4,20},{6,22},{8,24},{10,26},{12,28},{14,30},{16,0},... | collective-permute-start | bytes 221192 | tf_op jit(solution)/shard_map/ppermute | solution.py:79
  340.8 14.5 %collective-permute-start.27 = (bf16[48,768]{1,0:T(8,128)(2,1)S(1)}, bf16[48,768]{1,0:T(8,128)(2,1)S(1)}, u32[]{:S(2)}, u32[]{:S(2)}) collective-permute-start(bf16[48,768]{1,0:T(8,128)(2,1)S(1)} %slice.409), channel_id=1, source_target_pairs={{0,16},{2,18},{4,20},{6,22},{8,24},{10,26},{12,28},{14,30},{16,0},... | collective-permute-start | bytes 221192 | tf_op jit(solution)/shard_map/ppermute | solution.py:79
  368.5 9.3 %collective-permute-start.11 = (f32[2688]{0:T(1024)S(1)}, f32[2688]{0:T(1024)S(1)}, u32[]{:S(2)}, u32[]{:S(2)}) collective-permute-start(f32[2688]{0:T(1024)S(1)} %add.643), channel_id=1, source_target_pairs={{0,16},{2,18},{4,20},{6,22},{8,24},{10,26},{12,28},{14,30},{16,0},... | collective-permute-start | bytes 32264 | tf_op jit(solution)/shard_map/ppermute | solution.py:79
  371.5 8.0 %collective-permute-start.13 = (bf16[192,768]{0,1:T(8,128)(2,1)S(1)}, bf16[192,768]{0,1:T(8,128)(2,1)}, u32[]{:S(2)}, u32[]{:S(2)}) collective-permute-start(bf16[192,768]{0,1:T(8,128)(2,1)S(1)} %slice.376), channel_id=1, source_target_pairs={{0,4},{2,6},{4,0},{6,2},{8,12},{10,14},{12,8},{14,10},{16,20},{18,... | collective-permute-start | bytes 884744 | tf_op jit(solution)/shard_map/ppermute | solution.py:79
  374.8 7.8 %collective-permute-start.17 = (bf16[192,768]{1,0:T(8,128)(2,1)}, bf16[192,768]{1,0:T(8,128)(2,1)}, u32[]{:S(2)}, u32[]{:S(2)}) collective-permute-start(bf16[192,768]{1,0:T(8,128)(2,1)} %slice.385), channel_id=1, source_target_pairs={{0,2},{2,0},{4,6},{6,4},{8,10},{10,8},{12,14},{14,12},{16,18},{18,... | collective-permute-start | bytes 884744 | tf_op jit(solution)/shard_map/ppermute | solution.py:79
  383.7 13.0 %collective-permute-start.18 = (bf16[96,768]{1,0:T(8,128)(2,1)S(1)}, bf16[96,768]{1,0:T(8,128)(2,1)}, u32[]{:S(2)}, u32[]{:S(2)}) collective-permute-start(bf16[96,768]{1,0:T(8,128)(2,1)S(1)} %slice.387), channel_id=1, source_target_pairs={{0,8},{2,10},{4,12},{6,14},{8,0},{10,2},{12,4},{14,6},{16,24},{18,... | collective-permute-start | bytes 442376 | tf_op jit(solution)/shard_map/ppermute | solution.py:79
  388.6 20.3 %collective-permute-start.15 = (bf16[48,768]{0,1:T(8,128)(2,1)}, bf16[48,768]{0,1:T(8,128)(2,1)}, u32[]{:S(2)}, u32[]{:S(2)}) collective-permute-start(bf16[48,768]{0,1:T(8,128)(2,1)} %slice.380), channel_id=1, source_target_pairs={{0,16},{2,18},{4,20},{6,22},{8,24},{10,26},{12,28},{14,30},{16,0},... | collective-permute-start | bytes 221192 | tf_op jit(solution)/shard_map/ppermute | solution.py:79
  388.9 29.4 %all-to-all-start.2 = ((bf16[16,32,768]{2,1,0:T(8,128)(2,1)}), bf16[16,32,768]{2,1,0:T(8,128)(2,1)S(1)}, u32[]{:S(2)}, u32[]{:S(2)}) async-start(bf16[16,32,768]{2,1,0:T(8,128)(2,1)} %bitcast.34), calls=%async_computation.2 | async-start | bytes 1572864 | tf_op jit(solution)/shard_map/all_to_all | solution.py:71
  398.6 18.1 %collective-permute-start.19 = (bf16[48,768]{1,0:T(8,128)(2,1)}, bf16[48,768]{1,0:T(8,128)(2,1)}, u32[]{:S(2)}, u32[]{:S(2)}) collective-permute-start(bf16[48,768]{1,0:T(8,128)(2,1)} %slice.389), channel_id=1, source_target_pairs={{0,16},{2,18},{4,20},{6,22},{8,24},{10,26},{12,28},{14,30},{16,0},... | collective-permute-start | bytes 221192 | tf_op jit(solution)/shard_map/ppermute | solution.py:79
  (131 other events, 911.3 us)
